TPU v7x, 32 devices: a whole 2x2x4 slice. The times are simulated.
32 devices in a mesh: dom: 8 (over z, x), inst: 4 (over y, core).
Axes of the slice: x: 2, y: 2, z: 4, core: 2. Of those that a mesh axis runs over, the one named last changes fastest.
Arguments:
- state: float32 [5, 16, 4096], P(None, 'inst', 'dom'), may hold values from -0.65 to 3.75, as said below
- cell_volume: float32 [4096], P('dom'), may hold values from 1 to 4
- step_size: float32 [4096], P('dom'), may hold values from 0.02 to 0.1
- face_normal: float32 [3, 16384], P(None, 'dom'), may hold values from -1 to 1
- owner_arm: float32 [3, 16384], P(None, 'dom'), may hold values from -0.09 to 0.09
- neighbor_arm: float32 [3, 16384], P(None, 'dom'), may hold values from -0.09 to 0.09
- face_owner: int32 [16384], P('dom'), may hold values from 0 to 511, as said below
- face_neighbor: int32 [16384], P('dom'), may hold values from 0 to 767, as said below
- face_count: int32 [8], P('dom'), may hold values from 1024 to 2048, as said below
- send_cells: int32 [32, 64], P('dom'), may hold values from 0 to 511
Outputs:
- new_state: float32 [5, 16, 4096], P(None, 'inst', 'dom')
- residual: float32 [5, 16, 4096], P(None, 'inst', 'dom')
Inputs may be any that keep to these rules, and one draw needn't show every extreme that they name: The state is physical: density 0.7 to 1.3 and pressure 0.4 (E - |m|^2 / (2 rho)) 0.7 to 1.3. `face_owner`: local ids of cells of the face's own partition. `face_neighbor`: either a local cell id below 512, or the ghost id 512 + k * 64 + s of block k; blocks of partitions that do not exist are never named. `face_count`: live face slots come first in each partition; some partition has all 2048 slots live. `send_cells`: row 4 q + k lists cells of partition q that fill ghost block k of partition q - o_k, o = (-2, -1, 1, 2); slots that no face names are padding.
All inputs are finite; a program needn't handle non-finite values.
Results may differ from a plain program's by a relative error of at most 0.0003.
Values sent between devices are 32-bit elements; how exact they have to be, the bound alone decides.
A program may use at most 128 MiB of HBM per device.

v0:
```python
import functools

import jax
import jax.numpy as jnp
import numpy as np
from jax import lax
from jax.experimental import pallas as pl
from jax.experimental.pallas import tpu as pltpu
from jax.sharding import PartitionSpec as P

HEAT_RATIO = 1.4
FREQUENCY = 0.5
PEER_OFFSETS = (-2, -1, 1, 2)
MESH = pl.DeviceIdType.MESH
BF = jnp.bfloat16
F32 = jnp.float32


def spectral_matrix(points, inst_dev, nvar, rows):
    peers = points // inst_dev
    table = np.zeros((rows, peers * rows))
    for k in range(peers):
        for v in range(nvar):
            for t in range(inst_dev):
                for j in range(inst_dev):
                    d = (t - j - k * inst_dev) % points
                    if d:
                        table[v * inst_dev + t, k * rows + v * inst_dev + j] = (
                            0.5 * (-1.0) ** d / np.tan(np.pi * d / points)
                        )
    table = table.astype(np.float32)
    high = table.astype(jnp.bfloat16).astype(np.float32)
    low = table - high
    return np.concatenate([high, high, low], axis=1).astype(jnp.bfloat16)


def parts(x):
    high = x.astype(BF).astype(F32)
    return jnp.concatenate([x, x - high], axis=0).astype(BF)


def joined(y):
    half = y.shape[0] // 2
    return y[:half] + y[half:]


def mm(a, b):
    return lax.dot_general(a, b, (((1,), (0,)), ((), ())), preferred_element_type=F32)


def mm_nt(a, b):
    return lax.dot_general(a, b, (((1,), (1,)), ((), ())), preferred_element_type=F32)


def euler_flux(u, n, area):
    rho, m1, m2, m3, energy = u
    inv = 1.0 / rho
    u1, u2, u3 = m1 * inv, m2 * inv, m3 * inv
    pressure = (HEAT_RATIO - 1.0) * (energy - 0.5 * (m1 * u1 + m2 * u2 + m3 * u3))
    q = u1 * n[0] + u2 * n[1] + u3 * n[2]
    flux = (
        rho * q,
        m1 * q + pressure * n[0],
        m2 * q + pressure * n[1],
        m3 * q + pressure * n[2],
        (energy + pressure) * q,
    )
    speed = jnp.abs(q) + jnp.sqrt(HEAT_RATIO * pressure * inv) * area
    return flux, speed


def kernel(
    dims,
    state_ref, volume_ref, step_ref, normal_ref, oarm_ref, narm_ref, owner_ref, neighbor_ref,
    count_ref, send_ref, table_ref,
    new_ref, res_ref,
    own_ref, peer_ref, payv_ref, payg_ref, gv_ref, gg_ref,
    st_ref, ot_ref, nt_ref, pm_ref, dm_ref, left_ref, right_ref, acc_ref,
    sv_send, sv_recv, sg_send, sg_recv, sp_send, sp_recv,
):
    ndom, ninst, nvar, idev, cells, slots, chunks, chunk, rows = dims
    ghosts = 4 * slots
    me = lax.axis_index("dom")
    mi = lax.axis_index("inst")

    def valid(p):
        return (p >= 0) & (p < ndom)

    gv_ref[...] = jnp.zeros(gv_ref.shape, F32)
    gg_ref[...] = jnp.zeros(gg_ref.shape, F32)

    barrier = pltpu.get_barrier_semaphore()
    for off in PEER_OFFSETS:
        @pl.when(valid(me + off))
        def _(off=off):
            pl.semaphore_signal(barrier, inc=1, device_id={"dom": me + off}, device_id_type=MESH)
    for k in range(1, ninst):
        pl.semaphore_signal(
            barrier, inc=1, device_id={"inst": lax.rem(mi + k, ninst)}, device_id_type=MESH
        )

    def ghost_copy(pay, dst, send, recv, sec, k, partition):
        return pltpu.make_async_remote_copy(
            src_ref=pay.at[sec, k // 2],
            dst_ref=dst.at[sec, k],
            send_sem=send.at[sec, k],
            recv_sem=recv.at[sec, k],
            device_id={"dom": partition},
            device_id_type=MESH,
        )

    def ghosts_start(args, sec):
        for k, off in enumerate(PEER_OFFSETS):
            @pl.when(valid(me - off))
            def _(k=k, off=off):
                ghost_copy(*args, sec, k, me - off).start()

    def ghosts_wait(args, sec):
        for k, off in enumerate(PEER_OFFSETS):
            @pl.when(valid(me + off))
            def _(k=k, off=off):
                ghost_copy(*args, sec, k, me + off).wait_recv()

    def ghosts_sent(args, sec):
        for k, off in enumerate(PEER_OFFSETS):
            @pl.when(valid(me - off))
            def _(k=k, off=off):
                ghost_copy(*args, sec, k, me - off).wait_send()

    def peer_copy(sec, k):
        return pltpu.make_async_remote_copy(
            src_ref=own_ref.at[sec],
            dst_ref=peer_ref.at[sec, k - 1],
            send_sem=sp_send.at[sec, k - 1],
            recv_sem=sp_recv.at[sec, k - 1],
            device_id={"inst": lax.rem(mi + ninst - k, ninst)},
            device_id_type=MESH,
        )

    vargs = (payv_ref, gv_ref, sv_send, sv_recv)
    gargs = (payg_ref, gg_ref, sg_send, sg_recv)

    cell_id = lax.broadcasted_iota(jnp.int32, (cells, slots), 0)
    for k in range(4):
        hit = cell_id == send_ref[k:k + 1, :]
        st_ref[:, k * slots:(k + 1) * slots] = jnp.where(hit, 1.0, 0.0).astype(BF)

    pad = rows - nvar * idev
    filler = [jnp.zeros((pad, cells), F32)] if pad else []
    current = jnp.concatenate([state_ref[v] for v in range(nvar)] + filler, axis=0)
    own_ref[0] = current
    split = parts(current)

    def fill_payload(pay, sec, values):
        for j in range(2):
            pay[sec, j] = values[:, j * 2 * slots:(j + 1) * 2 * slots]

    fill_payload(payv_ref, 0, joined(mm(split, st_ref[...])))

    neighbours = sum(valid(me + off).astype(jnp.int32) for off in PEER_OFFSETS)
    pl.semaphore_wait(barrier, neighbours + (ninst - 1))

    ghosts_start(vargs, 0)
    for k in range(1, ninst):
        peer_copy(0, k).start()

    def build(c, carry):
        at = pl.ds(pl.multiple_of(c * chunk, chunk), chunk)
        ids = lax.broadcasted_iota(jnp.int32, (cells, chunk), 0)
        gids = lax.broadcasted_iota(jnp.int32, (ghosts, chunk), 0) + cells
        own = owner_ref[:, at]
        nbr = neighbor_ref[:, at]
        o = jnp.where(ids == own, 1.0, 0.0)
        n = jnp.where(ids == nbr, 1.0, 0.0)
        ot_ref[c] = o.astype(BF)
        nt_ref[c, :cells] = n.astype(BF)
        nt_ref[c, cells:] = jnp.where(gids == nbr, 1.0, 0.0).astype(BF)
        pm_ref[c] = (o + n).astype(BF)
        dm_ref[c] = (o - n).astype(BF)
        return carry

    lax.fori_loop(0, chunks, build, 0)

    inv_volume = 1.0 / volume_ref[...]
    lane = lax.broadcasted_iota(jnp.int32, (1, chunk), 1)
    half = chunk // 2
    low_rows = lax.broadcasted_iota(jnp.int32, (2 * idev, half), 0) < idev

    def packed(x, v):
        tile = x[(v // 2) * 2 * idev:(v // 2 + 1) * 2 * idev]
        a, b = tile[:, :half], tile[:, half:]
        if v % 2 == 0:
            return jnp.where(low_rows, a, pltpu.roll(b, idev, 0))
        return jnp.where(low_rows, pltpu.roll(a, idev, 0), b)

    def unpacked(even, odd):
        if odd is None:
            a = jnp.where(low_rows, even, 0.0)
            b = jnp.where(low_rows, pltpu.roll(even, idev, 0), 0.0)
        else:
            a = jnp.where(low_rows, even, pltpu.roll(odd, idev, 0))
            b = jnp.where(low_rows, pltpu.roll(even, idev, 0), odd)
        return jnp.concatenate([a, b], axis=1)

    def both_halves(x):
        return jnp.where(low_rows, x[:, :half], x[:, half:])

    def ghost_values(ref, sec):
        wide = ref.shape[-2]
        first = lax.broadcasted_iota(jnp.int32, (wide, 2 * slots), 1) < slots
        return jnp.concatenate(
            [jnp.where(first, ref[sec, 2 * j], ref[sec, 2 * j + 1]) for j in range(2)], axis=1
        )

    def section(sec, split):
        def gather_local(c, carry):
            left_ref[c] = joined(mm(split, ot_ref[c]))
            right_ref[c] = joined(mm(split, nt_ref[c, :cells]))
            return carry

        lax.fori_loop(0, chunks, gather_local, 0)
        ghosts_wait(vargs, sec)
        gsplit = parts(ghost_values(gv_ref, sec))
        acc_ref[...] = jnp.zeros(acc_ref.shape, F32)

        def gradient_step(c, carry):
            at = pl.ds(pl.multiple_of(c * chunk, chunk), chunk)
            right = right_ref[c] + joined(mm(gsplit, nt_ref[c, cells:]))
            right_ref[c] = right
            live = (lane + c * chunk) < count_ref[0]
            jump = jnp.where(live, 0.5 * (right - left_ref[c]), 0.0)
            flow = jnp.concatenate([jump * normal_ref[d:d + 1, at] for d in range(3)], axis=0)
            acc_ref[...] += joined(mm_nt(parts(flow), pm_ref[c]))
            return carry

        lax.fori_loop(0, chunks, gradient_step, 0)
        gradient = acc_ref[...] * inv_volume
        dsplit = parts(gradient)
        fill_payload(payg_ref, sec, joined(mm(dsplit, st_ref[...])))
        ghosts_start(gargs, sec)

        def reconstruct(c, carry):
            at = pl.ds(pl.multiple_of(c * chunk, chunk), chunk)
            left = joined(mm(dsplit, ot_ref[c]))
            right = joined(mm(dsplit, nt_ref[c, :cells]))
            tl, tr = left_ref[c], right_ref[c]
            for d in range(3):
                tl = tl + left[d * rows:(d + 1) * rows] * oarm_ref[d:d + 1, at]
                tr = tr + right[d * rows:(d + 1) * rows] * narm_ref[d:d + 1, at]
            left_ref[c] = tl
            right_ref[c] = tr
            return carry

        lax.fori_loop(0, chunks, reconstruct, 0)

        for k in range(1, ninst):
            peer_copy(sec, k).wait_recv()
        every = jnp.concatenate(
            [own_ref[sec]] + [peer_ref[sec, k - 1] for k in range(1, ninst)], axis=0
        )
        high = every.astype(BF).astype(F32)
        stacked = jnp.concatenate([every, every - high, every], axis=0).astype(BF)
        spectral = mm(table_ref[...], stacked)

        ghosts_wait(gargs, sec)
        hsplit = parts(ghost_values(gg_ref, sec))
        acc_ref[:rows] = jnp.zeros((rows, cells), F32)

        def flux_step(c, carry):
            at = pl.ds(pl.multiple_of(c * chunk, chunk), chunk)
            extra = joined(mm(hsplit, nt_ref[c, cells:]))
            tl, tr = left_ref[c], right_ref[c]
            for d in range(3):
                tr = tr + extra[d * rows:(d + 1) * rows] * narm_ref[d:d + 1, at]
            normals = [both_halves(normal_ref[d:d + 1, at]) for d in range(3)]
            area = jnp.sqrt(
                normals[0] * normals[0] + normals[1] * normals[1] + normals[2] * normals[2]
            )
            ul = [packed(tl, v) for v in range(nvar)]
            ur = [packed(tr, v) for v in range(nvar)]
            fl, sl = euler_flux(ul, normals, area)
            fr, sr = euler_flux(ur, normals, area)
            wave = jnp.maximum(sl, sr)
            flux = [
                0.5 * ((fl[v] + fr[v]) - wave * (ur[v] - ul[v])) for v in range(nvar)
            ] + [None]
            face = jnp.concatenate(
                [unpacked(flux[2 * j], flux[2 * j + 1]) for j in range((nvar + 1) // 2)], axis=0
            )
            live = (lane + c * chunk) < count_ref[0]
            face = jnp.where(live, face, 0.0)
            acc_ref[:rows] += joined(mm_nt(parts(face), dm_ref[c]))
            return carry

        lax.fori_loop(0, chunks, flux_step, 0)
        return acc_ref[:rows] * inv_volume + FREQUENCY * spectral

    step = step_ref[...]
    current = current - 0.5 * step * section(0, split)
    own_ref[1] = current
    for k in range(1, ninst):
        peer_copy(1, k).start()
    split = parts(current)
    fill_payload(payv_ref, 1, joined(mm(split, st_ref[...])))
    ghosts_start(vargs, 1)
    residual = section(1, split)
    new = own_ref[0] - step * residual
    for v in range(nvar):
        new_ref[v] = new[v * idev:(v + 1) * idev]
        res_ref[v] = residual[v * idev:(v + 1) * idev]

    for sec in range(2):
        ghosts_sent(vargs, sec)
        ghosts_sent(gargs, sec)
        for k in range(1, ninst):
            peer_copy(sec, k).wait_send()


def solution(mesh):
    ndom, ninst = mesh.shape["dom"], mesh.shape["inst"]

    def local(
        state, cell_volume, step_size, face_normal, owner_arm, neighbor_arm,
        face_owner, face_neighbor, face_count, send_cells,
    ):
        nvar, idev, cells = state.shape
        faces = face_owner.shape[0]
        slots = send_cells.shape[1]
        chunk = min(512, faces)
        chunks = faces // chunk
        rows = -(-nvar * idev // 8) * 8
        ghosts = 4 * slots
        dims = (ndom, ninst, nvar, idev, cells, slots, chunks, chunk, rows)
        table = jnp.asarray(spectral_matrix(idev * ninst, idev, nvar, rows))
        vmem = pl.BlockSpec(memory_space=pltpu.VMEM)
        smem = pl.BlockSpec(memory_space=pltpu.SMEM)
        shape = jax.ShapeDtypeStruct(state.shape, F32)
        dma = pltpu.SemaphoreType.DMA
        return pl.pallas_call(
            functools.partial(kernel, dims),
            out_shape=(shape, shape),
            in_specs=[vmem] * 8 + [smem] + [vmem] * 2,
            out_specs=(vmem, vmem),
            scratch_shapes=[
                pltpu.VMEM((2, rows, cells), F32),
                pltpu.VMEM((2, ninst - 1, rows, cells), F32),
                pltpu.VMEM((2, 2, rows, 2 * slots), F32),
                pltpu.VMEM((2, 2, 3 * rows, 2 * slots), F32),
                pltpu.VMEM((2, 4, rows, 2 * slots), F32),
                pltpu.VMEM((2, 4, 3 * rows, 2 * slots), F32),
                pltpu.VMEM((cells, ghosts), BF),
                pltpu.VMEM((chunks, cells, chunk), BF),
                pltpu.VMEM((chunks, cells + ghosts, chunk), BF),
                pltpu.VMEM((chunks, cells, chunk), BF),
                pltpu.VMEM((chunks, cells, chunk), BF),
                pltpu.VMEM((chunks, rows, chunk), F32),
                pltpu.VMEM((chunks, rows, chunk), F32),
                pltpu.VMEM((3 * rows, cells), F32),
                dma((2, 4)), dma((2, 4)), dma((2, 4)), dma((2, 4)),
                dma((2, ninst - 1)), dma((2, ninst - 1)),
            ],
            compiler_params=pltpu.CompilerParams(
                collective_id=0, has_side_effects=True, vmem_limit_bytes=40 * 1024 * 1024
            ),
        )(
            state, cell_volume[None], step_size[None], face_normal, owner_arm, neighbor_arm,
            face_owner[None], face_neighbor[None], face_count, send_cells, table,
        )

    placed = (
        P(None, "inst", "dom"),
        P("dom"),
        P("dom"),
        P(None, "dom"),
        P(None, "dom"),
        P(None, "dom"),
        P("dom"),
        P("dom"),
        P("dom"),
        P("dom", None),
    )
    return jax.shard_map(
        local,
        mesh=mesh,
        in_specs=placed,
        out_specs=(P(None, "inst", "dom"), P(None, "inst", "dom")),
        check_vma=False,
    )
```

profile of v0, /device:TPU:0, one launch (start us, length us, event | category | flops | bytes accessed | tf_op | source)
XLA Modules:
  0.0 34.7 jit_solution(13720861826750826901)
XLA Ops:
  0.6 0.0 copy-start.5
  1.3 0.0 copy-done.5
  1.3 0.0 copy-start
  1.3 0.8 %copy-done = f32[5,4,512]{2,1,0:T(4,128)S(1)} copy-done((f32[5,4,512]{2,1,0:T(4,128)S(1)}, f32[5,4,512]{2,1,0:T(4,128)}, u32[]{:S(2)}) %copy-start) | copy-done | bytes 40984
  2.1 0.0 copy-start.1
  2.1 0.8 %copy-done.1 = f32[3,2048]{1,0:T(4,128)S(1)} copy-done((f32[3,2048]{1,0:T(4,128)S(1)}, f32[3,2048]{1,0:T(4,128)}, u32[]{:S(2)}) %copy-start.1) | copy-done | bytes 24600
  2.9 0.0 copy-start.2
  2.9 0.8 %copy-done.2 = f32[3,2048]{1,0:T(4,128)S(1)} copy-done((f32[3,2048]{1,0:T(4,128)S(1)}, f32[3,2048]{1,0:T(4,128)}, u32[]{:S(2)}) %copy-start.2) | copy-done | bytes 24600
  3.6 0.0 copy-start.3
  3.6 0.8 %copy-done.3 = f32[3,2048]{1,0:T(4,128)S(1)} copy-done((f32[3,2048]{1,0:T(4,128)S(1)}, f32[3,2048]{1,0:T(4,128)}, u32[]{:S(2)}) %copy-start.3) | copy-done | bytes 24600
  4.4 0.0 copy-start.4
  4.4 0.7 %copy-done.4 = bf16[24,288]{1,0:T(8,128)(2,1)S(1)} copy-done((bf16[24,288]{1,0:T(8,128)(2,1)S(1)}, bf16[24,288]{1,0:T(8,128)(2,1)}, u32[]{:S(2)}) %copy-start.4) | copy-done | bytes 13848
  5.1 0.0 copy-start.6
  5.1 0.7 %copy-done.6 = s32[2048]{0:T(1024)S(1)} copy-done((s32[2048]{0:T(1024)S(1)}, s32[2048]{0:T(1024)}, u32[]{:S(2)}) %copy-start.6) | copy-done | bytes 8216
  5.8 0.0 copy-start.7
  5.8 0.7 %copy-done.7 = f32[512]{0:T(512)S(1)} copy-done((f32[512]{0:T(512)S(1)}, f32[512]{0:T(512)}, u32[]{:S(2)}) %copy-start.7) | copy-done | bytes 2072
  6.5 0.0 copy-start.8
  6.5 0.7 %copy-done.8 = f32[512]{0:T(512)S(1)} copy-done((f32[512]{0:T(512)S(1)}, f32[512]{0:T(512)}, u32[]{:S(2)}) %copy-start.8) | copy-done | bytes 2072
  7.2 0.0 copy-start.9
  7.2 0.7 %copy-done.9 = s32[4,64]{1,0:T(4,128)S(1)} copy-done((s32[4,64]{1,0:T(4,128)S(1)}, s32[4,64]{1,0:T(4,128)}, u32[]{:S(2)}) %copy-start.9) | copy-done | bytes 1048
  7.9 25.6 %shard_map.122 = (f32[5,4,512]{2,1,0:T(4,128)S(1)}, f32[5,4,512]{2,1,0:T(4,128)S(1)}) custom-call(f32[5,4,512]{2,1,0:T(4,128)S(1)} %copy-done, f32[1,512]{1,0:T(1,128)S(1)} %bitcast.6, f32[1,512]{1,0:T(1,128)S(1)} %bitcast.7, f32[3,2048]{1,0:T(4,128)S(1)} %copy-done.1, f32[3,2048]{1,0:T(4,128)S(1)} %copy-done.2, f32[3,2048]{1,0:T(4,128)S(1)} %copy-done.3, ...), custom_call_target="tpu_custom_call" | custom-call | tf_op jit(solution)/shard_map/pallas_call | solution.py:339
  33.4 0.6 %copy.16 = f32[5,4,512]{2,1,0:T(4,128)} copy(f32[5,4,512]{2,1,0:T(4,128)S(1)} %get-tuple-element.4) | data formatting | bytes 81920
  34.0 0.6 %copy.17 = f32[5,4,512]{2,1,0:T(4,128)} copy(f32[5,4,512]{2,1,0:T(4,128)S(1)} %get-tuple-element.5) | data formatting | bytes 81920
Async XLA Ops:
  0.6 0.7 %copy-start.5 = (s32[2048]{0:T(1024)S(1)}, s32[2048]{0:T(1024)}, u32[]{:S(2)}) copy-start(s32[2048]{0:T(1024)} %param.17) | copy-start | bytes 24580
  1.3 0.8 %copy-start = (f32[5,4,512]{2,1,0:T(4,128)S(1)}, f32[5,4,512]{2,1,0:T(4,128)}, u32[]{:S(2)}) copy-start(f32[5,4,512]{2,1,0:T(4,128)} %state_ref.1) | copy-start | bytes 122884
  2.1 0.8 %copy-start.1 = (f32[3,2048]{1,0:T(4,128)S(1)}, f32[3,2048]{1,0:T(4,128)}, u32[]{:S(2)}) copy-start(f32[3,2048]{1,0:T(4,128)} %normal_ref.1) | copy-start | bytes 73732
  2.9 0.8 %copy-start.2 = (f32[3,2048]{1,0:T(4,128)S(1)}, f32[3,2048]{1,0:T(4,128)}, u32[]{:S(2)}) copy-start(f32[3,2048]{1,0:T(4,128)} %oarm_ref.1) | copy-start | bytes 73732
  3.6 0.8 %copy-start.3 = (f32[3,2048]{1,0:T(4,128)S(1)}, f32[3,2048]{1,0:T(4,128)}, u32[]{:S(2)}) copy-start(f32[3,2048]{1,0:T(4,128)} %narm_ref.1) | copy-start | bytes 73732
  4.4 0.7 %copy-start.4 = (bf16[24,288]{1,0:T(8,128)(2,1)S(1)}, bf16[24,288]{1,0:T(8,128)(2,1)}, u32[]{:S(2)}) copy-start(bf16[24,288]{1,0:T(8,128)(2,1)} %constant.2.clone.table_ref) | copy-start | bytes 41476
  5.1 0.7 %copy-start.6 = (s32[2048]{0:T(1024)S(1)}, s32[2048]{0:T(1024)}, u32[]{:S(2)}) copy-start(s32[2048]{0:T(1024)} %param.18) | copy-start | bytes 24580
  5.8 0.7 %copy-start.7 = (f32[512]{0:T(512)S(1)}, f32[512]{0:T(512)}, u32[]{:S(2)}) copy-start(f32[512]{0:T(512)} %param.12) | copy-start | bytes 6148
  6.5 0.7 %copy-start.8 = (f32[512]{0:T(512)S(1)}, f32[512]{0:T(512)}, u32[]{:S(2)}) copy-start(f32[512]{0:T(512)} %param.13) | copy-start | bytes 6148
  7.2 0.7 %copy-start.9 = (s32[4,64]{1,0:T(4,128)S(1)}, s32[4,64]{1,0:T(4,128)}, u32[]{:S(2)}) copy-start(s32[4,64]{1,0:T(4,128)} %send_ref.1) | copy-start | bytes 3076
where the time goes:
time: 35.2 us; the launch traced here: 34.7 us
  Pallas kernels  25.6 us (73%)
  local copies, waits for them, and re-layouts  7.78 us (22%)
  between operations  1.32 us (4%)
    pallas_call x1, Pallas kernels, local(): pl.pallas_call(functools.partial(kernel, dims), out_shape=(shape, shape),...  25.6 us
    unnamed x22, local copies, waits for them, and re-layouts  7.78 us

commit v1 on v0

--- a/solution.py
+++ b/solution.py
@@ -71,9 +71,11 @@
 
 def kernel(
     dims,
+    state_hbm, volume_hbm, step_hbm, normal_hbm, oarm_hbm, narm_hbm, owner_hbm, neighbor_hbm,
+    count_hbm, send_hbm, table_hbm,
+    new_ref, res_ref,
     state_ref, volume_ref, step_ref, normal_ref, oarm_ref, narm_ref, owner_ref, neighbor_ref,
-    count_ref, send_ref, table_ref,
-    new_ref, res_ref,
+    count_ref, send_ref, table_ref, in_sem,
     own_ref, peer_ref, payv_ref, payg_ref, gv_ref, gg_ref,
     st_ref, ot_ref, nt_ref, pm_ref, dm_ref, left_ref, right_ref, acc_ref,
     sv_send, sv_recv, sg_send, sg_recv, sp_send, sp_recv,
@@ -86,6 +88,18 @@
     def valid(p):
         return (p >= 0) & (p < ndom)
 
+    fetches = [
+        pltpu.make_async_copy(source, target, in_sem.at[i])
+        for i, (source, target) in enumerate((
+            (state_hbm, state_ref), (send_hbm, send_ref),
+            (owner_hbm, owner_ref), (neighbor_hbm, neighbor_ref),
+            (volume_hbm, volume_ref), (count_hbm, count_ref), (normal_hbm, normal_ref),
+            (oarm_hbm, oarm_ref), (narm_hbm, narm_ref),
+            (step_hbm, step_ref), (table_hbm, table_ref),
+        ))
+    ]
+    for fetch in fetches:
+        fetch.start()
     gv_ref[...] = jnp.zeros(gv_ref.shape, F32)
     gg_ref[...] = jnp.zeros(gg_ref.shape, F32)
 
@@ -140,6 +154,8 @@
     vargs = (payv_ref, gv_ref, sv_send, sv_recv)
     gargs = (payg_ref, gg_ref, sg_send, sg_recv)
 
+    for fetch in fetches[:2]:
+        fetch.wait()
     cell_id = lax.broadcasted_iota(jnp.int32, (cells, slots), 0)
     for k in range(4):
         hit = cell_id == send_ref[k:k + 1, :]
@@ -164,19 +180,21 @@
     for k in range(1, ninst):
         peer_copy(0, k).start()
 
+    for fetch in fetches[2:]:
+        fetch.wait()
     def build(c, carry):
         at = pl.ds(pl.multiple_of(c * chunk, chunk), chunk)
         ids = lax.broadcasted_iota(jnp.int32, (cells, chunk), 0)
         gids = lax.broadcasted_iota(jnp.int32, (ghosts, chunk), 0) + cells
         own = owner_ref[:, at]
         nbr = neighbor_ref[:, at]
-        o = jnp.where(ids == own, 1.0, 0.0)
-        n = jnp.where(ids == nbr, 1.0, 0.0)
-        ot_ref[c] = o.astype(BF)
-        nt_ref[c, :cells] = n.astype(BF)
+        o = jnp.where(ids == own, 1.0, 0.0).astype(BF)
+        n = jnp.where(ids == nbr, 1.0, 0.0).astype(BF)
+        ot_ref[c] = o
+        nt_ref[c, :cells] = n
         nt_ref[c, cells:] = jnp.where(gids == nbr, 1.0, 0.0).astype(BF)
-        pm_ref[c] = (o + n).astype(BF)
-        dm_ref[c] = (o - n).astype(BF)
+        pm_ref[c] = o + n
+        dm_ref[c] = o - n
         return carry
 
     lax.fori_loop(0, chunks, build, 0)
@@ -227,7 +245,7 @@
             at = pl.ds(pl.multiple_of(c * chunk, chunk), chunk)
             right = right_ref[c] + joined(mm(gsplit, nt_ref[c, cells:]))
             right_ref[c] = right
-            live = (lane + c * chunk) < count_ref[0]
+            live = (lane + c * chunk) < count_ref[...]
             jump = jnp.where(live, 0.5 * (right - left_ref[c]), 0.0)
             flow = jnp.concatenate([jump * normal_ref[d:d + 1, at] for d in range(3)], axis=0)
             acc_ref[...] += joined(mm_nt(parts(flow), pm_ref[c]))
@@ -287,7 +305,7 @@
             face = jnp.concatenate(
                 [unpacked(flux[2 * j], flux[2 * j + 1]) for j in range((nvar + 1) // 2)], axis=0
             )
-            live = (lane + c * chunk) < count_ref[0]
+            live = (lane + c * chunk) < count_ref[...]
             face = jnp.where(live, face, 0.0)
             acc_ref[:rows] += joined(mm_nt(parts(face), dm_ref[c]))
             return carry
@@ -326,22 +344,34 @@
         nvar, idev, cells = state.shape
         faces = face_owner.shape[0]
         slots = send_cells.shape[1]
-        chunk = min(512, faces)
+        chunk = min(1024, faces)
         chunks = faces // chunk
         rows = -(-nvar * idev // 8) * 8
         ghosts = 4 * slots
         dims = (ndom, ninst, nvar, idev, cells, slots, chunks, chunk, rows)
         table = jnp.asarray(spectral_matrix(idev * ninst, idev, nvar, rows))
         vmem = pl.BlockSpec(memory_space=pltpu.VMEM)
-        smem = pl.BlockSpec(memory_space=pltpu.SMEM)
+        hbm = pl.BlockSpec(memory_space=pltpu.HBM)
         shape = jax.ShapeDtypeStruct(state.shape, F32)
         dma = pltpu.SemaphoreType.DMA
         return pl.pallas_call(
             functools.partial(kernel, dims),
             out_shape=(shape, shape),
-            in_specs=[vmem] * 8 + [smem] + [vmem] * 2,
+            in_specs=[hbm] * 11,
             out_specs=(vmem, vmem),
             scratch_shapes=[
+                pltpu.VMEM(state.shape, F32),
+                pltpu.VMEM((1, cells), F32),
+                pltpu.VMEM((1, cells), F32),
+                pltpu.VMEM((3, faces), F32),
+                pltpu.VMEM((3, faces), F32),
+                pltpu.VMEM((3, faces), F32),
+                pltpu.VMEM((1, faces), jnp.int32),
+                pltpu.VMEM((1, faces), jnp.int32),
+                pltpu.VMEM((1, 1), jnp.int32),
+                pltpu.VMEM((4, slots), jnp.int32),
+                pltpu.VMEM(table.shape, BF),
+                dma((11,)),
                 pltpu.VMEM((2, rows, cells), F32),
                 pltpu.VMEM((2, ninst - 1, rows, cells), F32),
                 pltpu.VMEM((2, 2, rows, 2 * slots), F32),
@@ -360,11 +390,11 @@
                 dma((2, ninst - 1)), dma((2, ninst - 1)),
             ],
             compiler_params=pltpu.CompilerParams(
-                collective_id=0, has_side_effects=True, vmem_limit_bytes=40 * 1024 * 1024
+                collective_id=0, has_side_effects=True, vmem_limit_bytes=64 * 1024 * 1024
             ),
         )(
             state, cell_volume[None], step_size[None], face_normal, owner_arm, neighbor_arm,
-            face_owner[None], face_neighbor[None], face_count, send_cells, table,
+            face_owner[None], face_neighbor[None], face_count[None], send_cells, table,
         )
 
     placed = (

time: 35.2 us -> 28 us (0.80)
  local copies, waits for them, and re-layouts: 7.78 us -> 2.03 us
  Pallas kernels: 25.6 us -> 24.4 us
    unnamed x22 -> x4, local copies, waits for them, and re-layouts: 7.78 us -> 2.03 us
    pallas_call x1, Pallas kernels: 25.6 us -> 24.4 us  [local(): pl.pallas_call(functools.partial(kernel, dims), out_shape=(shape, shape),...]
where the time goes in v1:
time: 28 us; the launch traced here: 27.7 us
  Pallas kernels  24.4 us (87%)
  local copies, waits for them, and re-layouts  2.03 us (7%)
  between operations  1.3 us (5%)
    pallas_call x1, Pallas kernels, local(): pl.pallas_call(functools.partial(kernel, dims), out_shape=(shape, shape),...  24.4 us
    unnamed x4, local copies, waits for them, and re-layouts  2.03 us

profile of v1, /device:TPU:0, one launch (start us, length us, event | category | flops | bytes accessed | tf_op | source)
XLA Modules:
  0.0 27.7 jit_solution(8522845320622204992)
XLA Ops:
  1.3 24.4 %shard_map.122 = (f32[5,4,512]{2,1,0:T(4,128)}, f32[5,4,512]{2,1,0:T(4,128)}) custom-call(f32[5,4,512]{2,1,0:T(4,128)} %state_hbm.1, f32[1,512]{1,0:T(1,128)} %bitcast.8, f32[1,512]{1,0:T(1,128)} %bitcast.9, f32[3,2048]{1,0:T(4,128)} %normal_hbm.1, f32[3,2048]{1,0:T(4,128)} %oarm_hbm.1, f32[3,2048]{1,0:T(4,128)} %narm_hbm.1, s32[1,2048]{1,0:T(1,128)} %bitcast.6, ...), custom_call_target="tpu_custom_call" | custom-call | tf_op jit(solution)/shard_map/pallas_call | solution.py:357
  25.7 0.0 copy-start
  25.7 1.4 %copy.16 = f32[5,4,512]{2,1,0:T(4,128)} copy(f32[5,4,512]{2,1,0:T(4,128)} %get-tuple-element.4) | data formatting | bytes 81920
  27.1 0.0 copy-done
  27.1 0.6 %copy.17 = f32[5,4,512]{2,1,0:T(4,128)} copy(f32[5,4,512]{2,1,0:T(4,128)S(1)} %copy-done) | data formatting | bytes 81920
Async XLA Ops:
  25.7 1.4 %copy-start = (f32[5,4,512]{2,1,0:T(4,128)S(1)}, f32[5,4,512]{2,1,0:T(4,128)}, u32[]{:S(2)}) copy-start(f32[5,4,512]{2,1,0:T(4,128)} %get-tuple-element.5) | copy-start | bytes 122884

commit v2 on v1

--- a/solution.py
+++ b/solution.py
@@ -344,7 +344,7 @@
         nvar, idev, cells = state.shape
         faces = face_owner.shape[0]
         slots = send_cells.shape[1]
-        chunk = min(1024, faces)
+        chunk = min(2048, faces)
         chunks = faces // chunk
         rows = -(-nvar * idev // 8) * 8
         ghosts = 4 * slots
@@ -390,12 +390,15 @@
                 dma((2, ninst - 1)), dma((2, ninst - 1)),
             ],
             compiler_params=pltpu.CompilerParams(
-                collective_id=0, has_side_effects=True, vmem_limit_bytes=64 * 1024 * 1024
+                collective_id=0, has_side_effects=True, vmem_limit_bytes=40 * 1024 * 1024
             ),
-        )(
-            state, cell_volume[None], step_size[None], face_normal, owner_arm, neighbor_arm,
-            face_owner[None], face_neighbor[None], face_count[None], send_cells, table,
-        )
+        )(*[
+            x if x.size == 1 else pltpu.with_memory_space_constraint(x, pltpu.HBM)
+            for x in (
+                state, cell_volume[None], step_size[None], face_normal, owner_arm, neighbor_arm,
+                face_owner[None], face_neighbor[None], face_count[None], send_cells, table,
+            )
+        ])
 
     placed = (
         P(None, "inst", "dom"),

time: 28 us -> 25.5 us (0.911)
  Pallas kernels: 24.4 us -> 22.8 us
  local copies, waits for them, and re-layouts: 2.03 us -> 1.24 us
    pallas_call x1, Pallas kernels: 24.4 us -> 22.8 us  [local(): pl.pallas_call(functools.partial(kernel, dims), out_shape=(shape, shape),...]
    unnamed x4 -> x2, local copies, waits for them, and re-layouts: 2.03 us -> 1.24 us
where the time goes in v2:
time: 25.5 us; the launch traced here: 25.3 us
  Pallas kernels  22.8 us (89%)
  between operations  1.29 us (5%)
  local copies, waits for them, and re-layouts  1.24 us (5%)
    pallas_call x1, Pallas kernels, local(): pl.pallas_call(functools.partial(kernel, dims), out_shape=(shape, shape),...  22.8 us
    unnamed x2, local copies, waits for them, and re-layouts  1.24 us

profile of v2, /device:TPU:0, one launch (start us, length us, event | category | flops | bytes accessed | tf_op | source)
XLA Modules:
  0.0 25.3 jit_solution(1364915877648220473)
XLA Ops:
  1.3 22.8 %shard_map.122 = (f32[5,4,512]{2,1,0:T(4,128)S(1)}, f32[5,4,512]{2,1,0:T(4,128)S(1)}) custom-call(f32[5,4,512]{2,1,0:T(4,128)} %state_hbm.1, f32[1,512]{1,0:T(1,128)} %bitcast.8, f32[1,512]{1,0:T(1,128)} %bitcast.9, f32[3,2048]{1,0:T(4,128)} %normal_hbm.1, f32[3,2048]{1,0:T(4,128)} %oarm_hbm.1, f32[3,2048]{1,0:T(4,128)} %narm_hbm.1, s32[1,2048]{1,0:T(1,128)} %bitcast.6, ...), custom_call_target="tpu_custom_call" | custom-call | tf_op jit(solution)/shard_map/pallas_call | solution.py:357
  24.1 0.6 %copy.16 = f32[5,4,512]{2,1,0:T(4,128)} copy(f32[5,4,512]{2,1,0:T(4,128)S(1)} %get-tuple-element.4) | data formatting | bytes 81920
  24.7 0.6 %copy.17 = f32[5,4,512]{2,1,0:T(4,128)} copy(f32[5,4,512]{2,1,0:T(4,128)S(1)} %get-tuple-element.5) | data formatting | bytes 81920

commit v3 on v2

--- a/solution.py
+++ b/solution.py
@@ -115,7 +115,7 @@
 
     def ghost_copy(pay, dst, send, recv, sec, k, partition):
         return pltpu.make_async_remote_copy(
-            src_ref=pay.at[sec, k // 2],
+            src_ref=pay.at[sec, k],
             dst_ref=dst.at[sec, k],
             send_sem=send.at[sec, k],
             recv_sem=recv.at[sec, k],
@@ -168,8 +168,13 @@
     split = parts(current)
 
     def fill_payload(pay, sec, values):
+        high = pay.shape[2]
+        first = lax.broadcasted_iota(jnp.int32, (high, 2 * slots), 1) < slots
         for j in range(2):
-            pay[sec, j] = values[:, j * 2 * slots:(j + 1) * 2 * slots]
+            pair = values[:, j * 2 * slots:(j + 1) * 2 * slots]
+            top, bottom = pair[:high], pair[pair.shape[0] - high:]
+            pay[sec, 2 * j] = jnp.where(first, top, pltpu.roll(bottom, slots, 1))
+            pay[sec, 2 * j + 1] = jnp.where(first, pltpu.roll(top, slots, 1), bottom)
 
     fill_payload(payv_ref, 0, joined(mm(split, st_ref[...])))
 
@@ -223,12 +228,16 @@
     def both_halves(x):
         return jnp.where(low_rows, x[:, :half], x[:, half:])
 
-    def ghost_values(ref, sec):
-        wide = ref.shape[-2]
-        first = lax.broadcasted_iota(jnp.int32, (wide, 2 * slots), 1) < slots
-        return jnp.concatenate(
-            [jnp.where(first, ref[sec, 2 * j], ref[sec, 2 * j + 1]) for j in range(2)], axis=1
-        )
+    def ghost_values(ref, sec, wide):
+        high = ref.shape[2]
+        first = lax.broadcasted_iota(jnp.int32, (high, 2 * slots), 1) < slots
+        pairs = []
+        for j in range(2):
+            a, b = ref[sec, 2 * j], ref[sec, 2 * j + 1]
+            top = jnp.where(first, a, pltpu.roll(b, slots, 1))
+            bottom = jnp.where(first, pltpu.roll(a, slots, 1), b)
+            pairs.append(jnp.concatenate([top, bottom[2 * high - wide:]], axis=0))
+        return jnp.concatenate(pairs, axis=1)
 
     def section(sec, split):
         def gather_local(c, carry):
@@ -238,7 +247,7 @@
 
         lax.fori_loop(0, chunks, gather_local, 0)
         ghosts_wait(vargs, sec)
-        gsplit = parts(ghost_values(gv_ref, sec))
+        gsplit = parts(ghost_values(gv_ref, sec, rows))
         acc_ref[...] = jnp.zeros(acc_ref.shape, F32)
 
         def gradient_step(c, carry):
@@ -281,7 +290,7 @@
         spectral = mm(table_ref[...], stacked)
 
         ghosts_wait(gargs, sec)
-        hsplit = parts(ghost_values(gg_ref, sec))
+        hsplit = parts(ghost_values(gg_ref, sec, 3 * rows))
         acc_ref[:rows] = jnp.zeros((rows, cells), F32)
 
         def flux_step(c, carry):
@@ -316,11 +325,11 @@
     step = step_ref[...]
     current = current - 0.5 * step * section(0, split)
     own_ref[1] = current
-    for k in range(1, ninst):
-        peer_copy(1, k).start()
     split = parts(current)
     fill_payload(payv_ref, 1, joined(mm(split, st_ref[...])))
     ghosts_start(vargs, 1)
+    for k in range(1, ninst):
+        peer_copy(1, k).start()
     residual = section(1, split)
     new = own_ref[0] - step * residual
     for v in range(nvar):
@@ -332,6 +341,17 @@
         ghosts_sent(gargs, sec)
         for k in range(1, ninst):
             peer_copy(sec, k).wait_send()
+
+
+def leave(new_ref, res_ref, new_out, res_out, sems):
+    copies = [
+        pltpu.make_async_copy(new_ref, new_out, sems.at[0]),
+        pltpu.make_async_copy(res_ref, res_out, sems.at[1]),
+    ]
+    for copy in copies:
+        copy.start()
+    for copy in copies:
+        copy.wait()
 
 
 def solution(mesh):
@@ -348,13 +368,15 @@
         chunks = faces // chunk
         rows = -(-nvar * idev // 8) * 8
         ghosts = 4 * slots
+        vhigh = -(-rows // 16) * 8
+        ghigh = -(-3 * rows // 16) * 8
         dims = (ndom, ninst, nvar, idev, cells, slots, chunks, chunk, rows)
         table = jnp.asarray(spectral_matrix(idev * ninst, idev, nvar, rows))
         vmem = pl.BlockSpec(memory_space=pltpu.VMEM)
         hbm = pl.BlockSpec(memory_space=pltpu.HBM)
         shape = jax.ShapeDtypeStruct(state.shape, F32)
         dma = pltpu.SemaphoreType.DMA
-        return pl.pallas_call(
+        results = pl.pallas_call(
             functools.partial(kernel, dims),
             out_shape=(shape, shape),
             in_specs=[hbm] * 11,
@@ -374,10 +396,10 @@
                 dma((11,)),
                 pltpu.VMEM((2, rows, cells), F32),
                 pltpu.VMEM((2, ninst - 1, rows, cells), F32),
-                pltpu.VMEM((2, 2, rows, 2 * slots), F32),
-                pltpu.VMEM((2, 2, 3 * rows, 2 * slots), F32),
-                pltpu.VMEM((2, 4, rows, 2 * slots), F32),
-                pltpu.VMEM((2, 4, 3 * rows, 2 * slots), F32),
+                pltpu.VMEM((2, 4, vhigh, 2 * slots), F32),
+                pltpu.VMEM((2, 4, ghigh, 2 * slots), F32),
+                pltpu.VMEM((2, 4, vhigh, 2 * slots), F32),
+                pltpu.VMEM((2, 4, ghigh, 2 * slots), F32),
                 pltpu.VMEM((cells, ghosts), BF),
                 pltpu.VMEM((chunks, cells, chunk), BF),
                 pltpu.VMEM((chunks, cells + ghosts, chunk), BF),
@@ -399,6 +421,13 @@
                 face_owner[None], face_neighbor[None], face_count[None], send_cells, table,
             )
         ])
+        return pl.pallas_call(
+            leave,
+            out_shape=(shape, shape),
+            in_specs=[vmem, vmem],
+            out_specs=(hbm, hbm),
+            scratch_shapes=[dma((2,))],
+        )(*results)
 
     placed = (
         P(None, "inst", "dom"),

time: 25.5 us -> 26.5 us (1.039)
  Pallas kernels: 22.8 us -> 23.7 us
    pallas_call x0 -> x1, Pallas kernels: none -> 1.44 us  [local(): pl.pallas_call(leave, out_shape=(shape, shape), in_specs=[vmem, vmem], ou...]
    pallas_call x1, Pallas kernels: 22.8 us -> 22.2 us  [local(): pl.pallas_call(functools.partial(kernel, dims), out_shape=(shape, shape),...]
    unnamed x2 -> x4, local copies, waits for them, and re-layouts: 1.24 us -> 1.22 us
where the time goes in v3:
time: 26.5 us; the launch traced here: 26.2 us
  Pallas kernels  23.7 us (89%)
  between operations  1.3 us (5%)
  local copies, waits for them, and re-layouts  1.22 us (5%)
    pallas_call x1, Pallas kernels, local(): pl.pallas_call(functools.partial(kernel, dims), out_shape=(shape, shape),...  22.2 us
    pallas_call x1, Pallas kernels, local(): pl.pallas_call(leave, out_shape=(shape, shape), in_specs=[vmem, vmem], ou...  1.44 us
    unnamed x4, local copies, waits for them, and re-layouts  1.22 us

profile of v3, /device:TPU:0, one launch (start us, length us, event | category | flops | bytes accessed | tf_op | source)
XLA Modules:
  0.0 26.2 jit_solution(10947720892606389998)
XLA Ops:
  1.3 22.2 %shard_map.122 = (f32[5,4,512]{2,1,0:T(4,128)S(1)}, f32[5,4,512]{2,1,0:T(4,128)S(1)}) custom-call(f32[5,4,512]{2,1,0:T(4,128)} %state_hbm.1, f32[1,512]{1,0:T(1,128)} %bitcast.8, f32[1,512]{1,0:T(1,128)} %bitcast.9, f32[3,2048]{1,0:T(4,128)} %normal_hbm.1, f32[3,2048]{1,0:T(4,128)} %oarm_hbm.1, f32[3,2048]{1,0:T(4,128)} %narm_hbm.1, s32[1,2048]{1,0:T(1,128)} %bitcast.6, ...), custom_call_target="tpu_custom_call" | custom-call | tf_op jit(solution)/shard_map/pallas_call | solution.py:379
  23.5 0.0 copy-start
  23.5 0.6 %copy-done = f32[5,4,512]{2,1,0:T(4,128)} copy-done((f32[5,4,512]{2,1,0:T(4,128)}, f32[5,4,512]{2,1,0:T(4,128)S(1)}, u32[]{:S(2)}) %copy-start) | copy-done | bytes 40984
  24.1 0.0 copy-start.1
  24.1 0.6 %copy-done.1 = f32[5,4,512]{2,1,0:T(4,128)} copy-done((f32[5,4,512]{2,1,0:T(4,128)}, f32[5,4,512]{2,1,0:T(4,128)S(1)}, u32[]{:S(2)}) %copy-start.1) | copy-done | bytes 40984
  24.8 1.4 %shard_map.123 = (f32[5,4,512]{2,1,0:T(4,128)}, f32[5,4,512]{2,1,0:T(4,128)}) custom-call(f32[5,4,512]{2,1,0:T(4,128)} %copy-done, f32[5,4,512]{2,1,0:T(4,128)} %copy-done.1), custom_call_target="tpu_custom_call" | custom-call | tf_op jit(solution)/shard_map/pallas_call | solution.py:424
Async XLA Ops:
  23.5 0.6 %copy-start = (f32[5,4,512]{2,1,0:T(4,128)}, f32[5,4,512]{2,1,0:T(4,128)S(1)}, u32[]{:S(2)}) copy-start(f32[5,4,512]{2,1,0:T(4,128)S(1)} %get-tuple-element.4.new_ref) | copy-start | bytes 122884
  24.1 0.6 %copy-start.1 = (f32[5,4,512]{2,1,0:T(4,128)}, f32[5,4,512]{2,1,0:T(4,128)S(1)}, u32[]{:S(2)}) copy-start(f32[5,4,512]{2,1,0:T(4,128)S(1)} %get-tuple-element.5.res_ref) | copy-start | bytes 122884

commit v4 on v3

--- a/solution.py
+++ b/solution.py
@@ -72,10 +72,10 @@
 def kernel(
     dims,
     state_hbm, volume_hbm, step_hbm, normal_hbm, oarm_hbm, narm_hbm, owner_hbm, neighbor_hbm,
-    count_hbm, send_hbm, table_hbm,
+    count_ref, send_hbm, table_hbm,
     new_ref, res_ref,
     state_ref, volume_ref, step_ref, normal_ref, oarm_ref, narm_ref, owner_ref, neighbor_ref,
-    count_ref, send_ref, table_ref, in_sem,
+    send_ref, table_ref, in_sem,
     own_ref, peer_ref, payv_ref, payg_ref, gv_ref, gg_ref,
     st_ref, ot_ref, nt_ref, pm_ref, dm_ref, left_ref, right_ref, acc_ref,
     sv_send, sv_recv, sg_send, sg_recv, sp_send, sp_recv,
@@ -93,7 +93,7 @@
         for i, (source, target) in enumerate((
             (state_hbm, state_ref), (send_hbm, send_ref),
             (owner_hbm, owner_ref), (neighbor_hbm, neighbor_ref),
-            (volume_hbm, volume_ref), (count_hbm, count_ref), (normal_hbm, normal_ref),
+            (volume_hbm, volume_ref), (normal_hbm, normal_ref),
             (oarm_hbm, oarm_ref), (narm_hbm, narm_ref),
             (step_hbm, step_ref), (table_hbm, table_ref),
         ))
@@ -189,17 +189,20 @@
         fetch.wait()
     def build(c, carry):
         at = pl.ds(pl.multiple_of(c * chunk, chunk), chunk)
-        ids = lax.broadcasted_iota(jnp.int32, (cells, chunk), 0)
-        gids = lax.broadcasted_iota(jnp.int32, (ghosts, chunk), 0) + cells
-        own = owner_ref[:, at]
-        nbr = neighbor_ref[:, at]
-        o = jnp.where(ids == own, 1.0, 0.0).astype(BF)
-        n = jnp.where(ids == nbr, 1.0, 0.0).astype(BF)
-        ot_ref[c] = o
-        nt_ref[c, :cells] = n
-        nt_ref[c, cells:] = jnp.where(gids == nbr, 1.0, 0.0).astype(BF)
-        pm_ref[c] = o + n
-        dm_ref[c] = o - n
+        ids = lax.broadcasted_iota(jnp.int16, (cells + ghosts, chunk), 0)
+        one, zero = jnp.ones((), BF), jnp.zeros((), BF)
+        own = owner_ref[:, at].astype(jnp.int16)
+        nbr = neighbor_ref[:, at].astype(jnp.int16)
+        ot_ref[c] = jnp.where(ids[:cells] == own, one, zero)
+        nt_ref[c] = jnp.where(ids == nbr, one, zero)
+        return carry
+
+    def build_sum(c, carry):
+        pm_ref[c] = ot_ref[c] + nt_ref[c, :cells]
+        return carry
+
+    def build_difference(c, carry):
+        dm_ref[c] = ot_ref[c] - nt_ref[c, :cells]
         return carry
 
     lax.fori_loop(0, chunks, build, 0)
@@ -246,6 +249,8 @@
             return carry
 
         lax.fori_loop(0, chunks, gather_local, 0)
+        if sec == 0:
+            lax.fori_loop(0, chunks, build_sum, 0)
         ghosts_wait(vargs, sec)
         gsplit = parts(ghost_values(gv_ref, sec, rows))
         acc_ref[...] = jnp.zeros(acc_ref.shape, F32)
@@ -254,7 +259,7 @@
             at = pl.ds(pl.multiple_of(c * chunk, chunk), chunk)
             right = right_ref[c] + joined(mm(gsplit, nt_ref[c, cells:]))
             right_ref[c] = right
-            live = (lane + c * chunk) < count_ref[...]
+            live = (lane + c * chunk) < count_ref[0]
             jump = jnp.where(live, 0.5 * (right - left_ref[c]), 0.0)
             flow = jnp.concatenate([jump * normal_ref[d:d + 1, at] for d in range(3)], axis=0)
             acc_ref[...] += joined(mm_nt(parts(flow), pm_ref[c]))
@@ -279,6 +284,8 @@
             return carry
 
         lax.fori_loop(0, chunks, reconstruct, 0)
+        if sec == 0:
+            lax.fori_loop(0, chunks, build_difference, 0)
 
         for k in range(1, ninst):
             peer_copy(sec, k).wait_recv()
@@ -314,7 +321,7 @@
             face = jnp.concatenate(
                 [unpacked(flux[2 * j], flux[2 * j + 1]) for j in range((nvar + 1) // 2)], axis=0
             )
-            live = (lane + c * chunk) < count_ref[...]
+            live = (lane + c * chunk) < count_ref[0]
             face = jnp.where(live, face, 0.0)
             acc_ref[:rows] += joined(mm_nt(parts(face), dm_ref[c]))
             return carry
@@ -341,17 +348,6 @@
         ghosts_sent(gargs, sec)
         for k in range(1, ninst):
             peer_copy(sec, k).wait_send()
-
-
-def leave(new_ref, res_ref, new_out, res_out, sems):
-    copies = [
-        pltpu.make_async_copy(new_ref, new_out, sems.at[0]),
-        pltpu.make_async_copy(res_ref, res_out, sems.at[1]),
-    ]
-    for copy in copies:
-        copy.start()
-    for copy in copies:
-        copy.wait()
 
 
 def solution(mesh):
@@ -376,10 +372,10 @@
         hbm = pl.BlockSpec(memory_space=pltpu.HBM)
         shape = jax.ShapeDtypeStruct(state.shape, F32)
         dma = pltpu.SemaphoreType.DMA
-        results = pl.pallas_call(
+        return pl.pallas_call(
             functools.partial(kernel, dims),
             out_shape=(shape, shape),
-            in_specs=[hbm] * 11,
+            in_specs=[hbm] * 8 + [pl.BlockSpec(memory_space=pltpu.SMEM)] + [hbm] * 2,
             out_specs=(vmem, vmem),
             scratch_shapes=[
                 pltpu.VMEM(state.shape, F32),
@@ -390,10 +386,9 @@
                 pltpu.VMEM((3, faces), F32),
                 pltpu.VMEM((1, faces), jnp.int32),
                 pltpu.VMEM((1, faces), jnp.int32),
-                pltpu.VMEM((1, 1), jnp.int32),
                 pltpu.VMEM((4, slots), jnp.int32),
                 pltpu.VMEM(table.shape, BF),
-                dma((11,)),
+                dma((10,)),
                 pltpu.VMEM((2, rows, cells), F32),
                 pltpu.VMEM((2, ninst - 1, rows, cells), F32),
                 pltpu.VMEM((2, 4, vhigh, 2 * slots), F32),
@@ -418,16 +413,9 @@
             x if x.size == 1 else pltpu.with_memory_space_constraint(x, pltpu.HBM)
             for x in (
                 state, cell_volume[None], step_size[None], face_normal, owner_arm, neighbor_arm,
-                face_owner[None], face_neighbor[None], face_count[None], send_cells, table,
+                face_owner[None], face_neighbor[None], face_count, send_cells, table,
             )
         ])
-        return pl.pallas_call(
-            leave,
-            out_shape=(shape, shape),
-            in_specs=[vmem, vmem],
-            out_specs=(hbm, hbm),
-            scratch_shapes=[dma((2,))],
-        )(*results)
 
     placed = (
         P(None, "inst", "dom"),

time: 26.5 us -> 25 us (0.943)
  Pallas kernels: 23.7 us -> 22.2 us
    pallas_call x1 -> x0, Pallas kernels: 1.44 us -> none  [local(): pl.pallas_call(leave, out_shape=(shape, shape), in_specs=[vmem, vmem], ou...]
    unnamed x4 -> x2, local copies, waits for them, and re-layouts: 1.22 us -> 1.24 us
where the time goes in v4:
time: 25 us; the launch traced here: 24.8 us
  Pallas kernels  22.2 us (89%)
  between operations  1.29 us (5%)
  local copies, waits for them, and re-layouts  1.24 us (5%)
    pallas_call x1, Pallas kernels, local(): pl.pallas_call(functools.partial(kernel, dims), out_shape=(shape, shape),...  22.2 us
    unnamed x2, local copies, waits for them, and re-layouts  1.24 us

profile of v4, /device:TPU:0, one launch (start us, length us, event | category | flops | bytes accessed | tf_op | source)
XLA Modules:
  0.0 24.8 jit_solution(3605397921051139523)
XLA Ops:
  1.3 22.2 %shard_map.122 = (f32[5,4,512]{2,1,0:T(4,128)S(1)}, f32[5,4,512]{2,1,0:T(4,128)S(1)}) custom-call(f32[5,4,512]{2,1,0:T(4,128)} %state_hbm.1, f32[1,512]{1,0:T(1,128)} %bitcast.6, f32[1,512]{1,0:T(1,128)} %bitcast.7, f32[3,2048]{1,0:T(4,128)} %normal_hbm.1, f32[3,2048]{1,0:T(4,128)} %oarm_hbm.1, f32[3,2048]{1,0:T(4,128)} %narm_hbm.1, s32[1,2048]{1,0:T(1,128)} %bitcast.4, ...), custom_call_target="tpu_custom_call" | custom-call | tf_op jit(solution)/shard_map/pallas_call | solution.py:375
  23.5 0.6 %copy.16 = f32[5,4,512]{2,1,0:T(4,128)} copy(f32[5,4,512]{2,1,0:T(4,128)S(1)} %get-tuple-element.4) | data formatting | bytes 81920
  24.2 0.6 %copy.17 = f32[5,4,512]{2,1,0:T(4,128)} copy(f32[5,4,512]{2,1,0:T(4,128)S(1)} %get-tuple-element.5) | data formatting | bytes 81920

commit v5 on v4

--- a/solution.py
+++ b/solution.py
@@ -48,10 +48,6 @@
     return lax.dot_general(a, b, (((1,), (0,)), ((), ())), preferred_element_type=F32)
 
 
-def mm_nt(a, b):
-    return lax.dot_general(a, b, (((1,), (1,)), ((), ())), preferred_element_type=F32)
-
-
 def euler_flux(u, n, area):
     rho, m1, m2, m3, energy = u
     inv = 1.0 / rho
@@ -198,11 +194,11 @@
         return carry
 
     def build_sum(c, carry):
-        pm_ref[c] = ot_ref[c] + nt_ref[c, :cells]
+        pm_ref[c] = jnp.transpose(ot_ref[c] + nt_ref[c, :cells])
         return carry
 
     def build_difference(c, carry):
-        dm_ref[c] = ot_ref[c] - nt_ref[c, :cells]
+        dm_ref[c] = jnp.transpose(ot_ref[c] - nt_ref[c, :cells])
         return carry
 
     lax.fori_loop(0, chunks, build, 0)
@@ -262,7 +258,7 @@
             live = (lane + c * chunk) < count_ref[0]
             jump = jnp.where(live, 0.5 * (right - left_ref[c]), 0.0)
             flow = jnp.concatenate([jump * normal_ref[d:d + 1, at] for d in range(3)], axis=0)
-            acc_ref[...] += joined(mm_nt(parts(flow), pm_ref[c]))
+            acc_ref[...] += joined(mm(parts(flow), pm_ref[c]))
             return carry
 
         lax.fori_loop(0, chunks, gradient_step, 0)
@@ -323,7 +319,7 @@
             )
             live = (lane + c * chunk) < count_ref[0]
             face = jnp.where(live, face, 0.0)
-            acc_ref[:rows] += joined(mm_nt(parts(face), dm_ref[c]))
+            acc_ref[:rows] += joined(mm(parts(face), dm_ref[c]))
             return carry
 
         lax.fori_loop(0, chunks, flux_step, 0)
@@ -398,8 +394,8 @@
                 pltpu.VMEM((cells, ghosts), BF),
                 pltpu.VMEM((chunks, cells, chunk), BF),
                 pltpu.VMEM((chunks, cells + ghosts, chunk), BF),
-                pltpu.VMEM((chunks, cells, chunk), BF),
-                pltpu.VMEM((chunks, cells, chunk), BF),
+                pltpu.VMEM((chunks, chunk, cells), BF),
+                pltpu.VMEM((chunks, chunk, cells), BF),
                 pltpu.VMEM((chunks, rows, chunk), F32),
                 pltpu.VMEM((chunks, rows, chunk), F32),
                 pltpu.VMEM((3 * rows, cells), F32),

time: 25 us -> 23.7 us (0.948)
  Pallas kernels: 22.2 us -> 21 us
    pallas_call x1, Pallas kernels: 22.2 us -> 21 us  [local(): pl.pallas_call(functools.partial(kernel, dims), out_shape=(shape, shape),...]
where the time goes in v5:
time: 23.7 us; the launch traced here: 23.5 us
  Pallas kernels  21 us (89%)
  between operations  1.29 us (5%)
  local copies, waits for them, and re-layouts  1.24 us (5%)
    pallas_call x1, Pallas kernels, local(): pl.pallas_call(functools.partial(kernel, dims), out_shape=(shape, shape),...  21 us
    unnamed x2, local copies, waits for them, and re-layouts  1.24 us

profile of v5, /device:TPU:0, one launch (start us, length us, event | category | flops | bytes accessed | tf_op | source)
XLA Modules:
  0.0 23.5 jit_solution(17085237868659027435)
XLA Ops:
  1.3 21.0 %shard_map.122 = (f32[5,4,512]{2,1,0:T(4,128)S(1)}, f32[5,4,512]{2,1,0:T(4,128)S(1)}) custom-call(f32[5,4,512]{2,1,0:T(4,128)} %state_hbm.1, f32[1,512]{1,0:T(1,128)} %bitcast.6, f32[1,512]{1,0:T(1,128)} %bitcast.7, f32[3,2048]{1,0:T(4,128)} %normal_hbm.1, f32[3,2048]{1,0:T(4,128)} %oarm_hbm.1, f32[3,2048]{1,0:T(4,128)} %narm_hbm.1, s32[1,2048]{1,0:T(1,128)} %bitcast.4, ...), custom_call_target="tpu_custom_call" | custom-call | tf_op jit(solution)/shard_map/pallas_call | solution.py:371
  22.3 0.6 %copy.16 = f32[5,4,512]{2,1,0:T(4,128)} copy(f32[5,4,512]{2,1,0:T(4,128)S(1)} %get-tuple-element.4) | data formatting | bytes 81920
  22.9 0.6 %copy.17 = f32[5,4,512]{2,1,0:T(4,128)} copy(f32[5,4,512]{2,1,0:T(4,128)S(1)} %get-tuple-element.5) | data formatting | bytes 81920

commit v6 on v5

--- a/solution.py
+++ b/solution.py
@@ -201,7 +201,7 @@
         dm_ref[c] = jnp.transpose(ot_ref[c] - nt_ref[c, :cells])
         return carry
 
-    lax.fori_loop(0, chunks, build, 0)
+    lax.fori_loop(0, chunks, build, 0, unroll=True)
 
     inv_volume = 1.0 / volume_ref[...]
     lane = lax.broadcasted_iota(jnp.int32, (1, chunk), 1)
@@ -244,9 +244,9 @@
             right_ref[c] = joined(mm(split, nt_ref[c, :cells]))
             return carry
 
-        lax.fori_loop(0, chunks, gather_local, 0)
+        lax.fori_loop(0, chunks, gather_local, 0, unroll=True)
         if sec == 0:
-            lax.fori_loop(0, chunks, build_sum, 0)
+            lax.fori_loop(0, chunks, build_sum, 0, unroll=True)
         ghosts_wait(vargs, sec)
         gsplit = parts(ghost_values(gv_ref, sec, rows))
         acc_ref[...] = jnp.zeros(acc_ref.shape, F32)
@@ -261,7 +261,7 @@
             acc_ref[...] += joined(mm(parts(flow), pm_ref[c]))
             return carry
 
-        lax.fori_loop(0, chunks, gradient_step, 0)
+        lax.fori_loop(0, chunks, gradient_step, 0, unroll=True)
         gradient = acc_ref[...] * inv_volume
         dsplit = parts(gradient)
         fill_payload(payg_ref, sec, joined(mm(dsplit, st_ref[...])))
@@ -279,9 +279,9 @@
             right_ref[c] = tr
             return carry
 
-        lax.fori_loop(0, chunks, reconstruct, 0)
+        lax.fori_loop(0, chunks, reconstruct, 0, unroll=True)
         if sec == 0:
-            lax.fori_loop(0, chunks, build_difference, 0)
+            lax.fori_loop(0, chunks, build_difference, 0, unroll=True)
 
         for k in range(1, ninst):
             peer_copy(sec, k).wait_recv()
@@ -322,7 +322,7 @@
             acc_ref[:rows] += joined(mm(parts(face), dm_ref[c]))
             return carry
 
-        lax.fori_loop(0, chunks, flux_step, 0)
+        lax.fori_loop(0, chunks, flux_step, 0, unroll=True)
         return acc_ref[:rows] * inv_volume + FREQUENCY * spectral
 
     step = step_ref[...]
@@ -356,7 +356,7 @@
         nvar, idev, cells = state.shape
         faces = face_owner.shape[0]
         slots = send_cells.shape[1]
-        chunk = min(2048, faces)
+        chunk = min(512, faces)
         chunks = faces // chunk
         rows = -(-nvar * idev // 8) * 8
         ghosts = 4 * slots

time: 23.7 us -> 25.5 us (1.076)
  Pallas kernels: 21 us -> 22.8 us
    pallas_call x1, Pallas kernels: 21 us -> 22.8 us  [local(): pl.pallas_call(functools.partial(kernel, dims), out_shape=(shape, shape),...]
where the time goes in v6:
time: 25.5 us; the launch traced here: 25.3 us
  Pallas kernels  22.8 us (89%)
  between operations  1.29 us (5%)
  local copies, waits for them, and re-layouts  1.24 us (5%)
    pallas_call x1, Pallas kernels, local(): pl.pallas_call(functools.partial(kernel, dims), out_shape=(shape, shape),...  22.8 us
    unnamed x2, local copies, waits for them, and re-layouts  1.24 us

profile of v6, /device:TPU:0, one launch (start us, length us, event | category | flops | bytes accessed | tf_op | source)
XLA Modules:
  0.0 25.3 jit_solution(10926128191678130698)
XLA Ops:
  1.3 22.8 %shard_map.122 = (f32[5,4,512]{2,1,0:T(4,128)S(1)}, f32[5,4,512]{2,1,0:T(4,128)S(1)}) custom-call(f32[5,4,512]{2,1,0:T(4,128)} %state_hbm.1, f32[1,512]{1,0:T(1,128)} %bitcast.6, f32[1,512]{1,0:T(1,128)} %bitcast.7, f32[3,2048]{1,0:T(4,128)} %normal_hbm.1, f32[3,2048]{1,0:T(4,128)} %oarm_hbm.1, f32[3,2048]{1,0:T(4,128)} %narm_hbm.1, s32[1,2048]{1,0:T(1,128)} %bitcast.4, ...), custom_call_target="tpu_custom_call" | custom-call | tf_op jit(solution)/shard_map/pallas_call | solution.py:371
  24.1 0.6 %copy.16 = f32[5,4,512]{2,1,0:T(4,128)} copy(f32[5,4,512]{2,1,0:T(4,128)S(1)} %get-tuple-element.4) | data formatting | bytes 81920
  24.7 0.6 %copy.17 = f32[5,4,512]{2,1,0:T(4,128)} copy(f32[5,4,512]{2,1,0:T(4,128)S(1)} %get-tuple-element.5) | data formatting | bytes 81920
